TPU v7x, 256 devices: a whole 4x4x8 slice. The times are simulated.
256 devices in a mesh: dom: 8 (over z), row: 16 (over y, x), col: 2 (over core).
Axes of the slice: x: 4, y: 4, z: 8, core: 2. Of those that a mesh axis runs over, the one named last changes fastest.
Arguments:
- next_inverse: bfloat16 [8, 4096, 4096], P('dom', 'row', 'col'), may hold values from -6 to 6
- next_arrow: bfloat16 [8, 64, 4096], P('dom', None, 'row'), may hold values from -6 to 6
- factor_win: bfloat16 [8, 4096, 3072], P('dom', 'row', 'col'), may hold values from -0.09375 to 0.09375
- factor_rest: bfloat16 [8, 4096, 1024], P('dom', 'row', 'col'), may hold values from -0.09375 to 0.09375
- arrow_win: bfloat16 [8, 64, 3072], P('dom', None, 'col'), may hold values from -0.75 to 0.75
- arrow_rest: bfloat16 [8, 64, 1024], P('dom', None, 'col'), may hold values from -0.75 to 0.75
- tip_inverse: bfloat16 [64, 64], replicated, may hold values from -6 to 6
- base_win: bfloat16 [8, 3072, 3072], P('dom', 'row', 'col'), may hold values from -6 to 6
- base_rest: bfloat16 [8, 3072, 1024], P('dom', 'row', 'col'), may hold values from -6 to 6
Outputs:
- sub_inverse: bfloat16 [8, 4096, 3072], P('dom', 'row', 'col')
- arrow_inverse: bfloat16 [8, 64, 3072], P('dom', None, 'col')
- diag_win: bfloat16 [8, 3072, 3072], P('dom', 'row', 'col')
- diag_rest: bfloat16 [8, 3072, 1024], P('dom', 'row', 'col')
All inputs are finite; a program needn't handle non-finite values.
Results may differ from a plain program's by a relative error of at most 0.0046.
Values may be sent and summed in bfloat16 or wider, within the bound.
A program may use at most 128 MiB of HBM per device.

v0:
```python
import jax
import jax.numpy as jnp
from jax import lax
from jax.sharding import PartitionSpec as P


def shifted(value, axis, steps):
    count = lax.axis_size(axis)
    leading, last = (max(0, -steps), min(count, count - steps))
    return lax.ppermute(value, axis, [(source, source + steps) for source in range(leading, last)])


def contract_first(left, right):
    return lax.dot_general(
        left, right, (((0,), (0,)), ((), ())), preferred_element_type=jnp.float32
    )


def per_device(
    next_inverse,
    next_arrow,
    factor_win,
    factor_rest,
    arrow_win,
    arrow_rest,
    tip_inverse,
    base_win,
    base_rest,
):
    inverse_tile = next_inverse[0]
    arrow_tile = next_arrow[0]
    factor_tile = factor_win[0]
    factor_other = factor_rest[0]
    ratio_tile = arrow_win[0]
    ratio_other = arrow_rest[0]
    factor_column = lax.all_gather(factor_tile, "row", axis=0, tiled=True)
    inverse_next, arrow_next = shifted((inverse_tile, arrow_tile), "dom", -1)
    start_sum = contract_first(arrow_next, ratio_tile)
    x_total = start_sum + jnp.dot(
        lax.all_gather(inverse_next, "col", axis=1, tiled=True),
        factor_column,
        preferred_element_type=jnp.float32,
    )
    x_bf = x_total.astype(jnp.bfloat16)
    y_part = jnp.dot(arrow_next, factor_tile, preferred_element_type=jnp.float32)
    y_total = lax.psum(y_part, "row") + jnp.dot(
        tip_inverse, ratio_tile, preferred_element_type=jnp.float32
    )
    y_bf = y_total.astype(jnp.bfloat16)
    x_panel, y_panel = (
        lax.all_gather(x_bf, "col", axis=1, tiled=True),
        lax.all_gather(y_bf, "col", axis=1, tiled=True),
    )
    ratio_both = jnp.concatenate([ratio_tile, ratio_other], axis=1)
    rows_here = y_panel.shape[1] // lax.axis_size("row")
    y_rows = lax.dynamic_slice_in_dim(y_panel, lax.axis_index("row") * rows_here, rows_here, 1)
    x_columns = lax.all_to_all(x_panel, "row", split_axis=1, concat_axis=0, tiled=True)
    rest_column = lax.all_gather(factor_other, "row", axis=0, tiled=True)
    factor_full = jnp.concatenate([factor_column, rest_column], axis=1)
    diag_part = contract_first(x_columns, factor_full)
    base_both = jnp.concatenate([base_win[0], base_rest[0]], axis=1).astype(jnp.float32)
    diag_total = base_both + diag_part + contract_first(y_rows, ratio_both)
    split = factor_tile.shape[1]
    diag_left = diag_total[:, :split].astype(jnp.bfloat16)
    diag_right = diag_total[:, split:].astype(jnp.bfloat16)
    return ((-x_bf)[None], (-y_bf)[None], diag_left[None], diag_right[None])


def solution(mesh):
    in_specs = (
        P("dom", "row", "col"),
        P("dom", None, "row"),
        P("dom", "row", "col"),
        P("dom", "row", "col"),
        P("dom", None, "col"),
        P("dom", None, "col"),
        P(),
        P("dom", "row", "col"),
        P("dom", "row", "col"),
    )
    out_specs = (
        P("dom", "row", "col"),
        P("dom", None, "col"),
        P("dom", "row", "col"),
        P("dom", "row", "col"),
    )
    return jax.shard_map(
        per_device, mesh=mesh, in_specs=in_specs, out_specs=out_specs, check_vma=False
    )
```

profile of v0, /device:TPU:104, one launch (start us, length us, event | category | flops | bytes accessed | tf_op | source)
XLA Modules:
  0.0 358.2 jit_solution(10407591954021950761)
XLA Ops:
  7.2 0.0 copy-start
  7.2 0.0 copy-start.7
  7.2 0.0 all-gather.7.cloned.1.call-start
  7.2 2.0 collective-permute-start.1
  9.3 26.4 %collective-permute-done.1 = bf16[256,2048]{1,0:T(8,128)(2,1)S(1)} collective-permute-done((bf16[256,2048]{1,0:T(8,128)(2,1)}, bf16[256,2048]{1,0:T(8,128)(2,1)S(1)}, u32[]{:S(2)}, u32[]{:S(2)}) %collective-permute-start.1) | collective-permute-done | bytes 1048608 | tf_op jit(solution)/shard_map/ppermute | solution.py:10
  35.6 0.0 copy-start.4
  35.6 1.0 copy-done.4
  36.6 0.0 all-gather.7.cloned.1.call-update
  36.7 0.0 all-gather.11.cloned.1.call-start
  36.7 0.7 all-gather.11.cloned.1.call-update
  37.4 0.0 all-gather.9.cloned.1.call-start
  37.5 0.0 copy-done.7
  37.5 0.0 copy-start.3
  37.5 2.1 collective-permute-start
  39.5 13.6 %all-gather.7.cloned.1.call-done = bf16[256,4096]{1,0:T(8,128)(2,1)} async-done(((bf16[256,2048]{1,0:T(8,128)(2,1)}), bf16[256,4096]{1,0:T(8,128)(2,1)}) %all-gather.7.cloned.1.call-update) | async-done | bytes 2097168 | tf_op jit(solution)/shard_map/all_gather | solution.py:40
  53.1 98.7 %all-gather.11.cloned.1.call-done = bf16[1,4096,1536]{2,1,0:T(8,128)(2,1)} async-done(((bf16[1,256,1536]{2,1,0:T(8,128)(2,1)}), bf16[1,4096,1536]{2,1,0:T(8,128)(2,1)}) %all-gather.11.cloned.1.call-update) | async-done | bytes 12582928 | tf_op jit(solution)/shard_map/all_gather | solution.py:36
  151.8 7.0 %fusion.18 = f32[256,1536]{1,0:T(8,128)S(1)} fusion(bf16[256,4096]{1,0:T(8,128)(2,1)} %all-gather.7.cloned.1.call-done, bf16[1,4096,1536]{2,1,0:T(8,128)(2,1)} %all-gather.11.cloned.1.call-done), kind=kOutput, calls=%fused_computation.23 | convolution fusion | flops 3221225472 | bytes 16252928 | tf_op jit(solution)/shard_map/dot_general | solution.py:39
  158.9 0.0 copy-start.2
  158.9 0.0 collective-permute-done
  158.9 0.0 copy-done.3
  158.9 1.3 fusion.4
  160.2 0.0 all-gather.9.cloned.1.call-update
  160.2 0.0 all-reduce.2.cloned.1.call-start
  160.2 0.0 copy-done.2
  160.3 1.0 fusion.9
  161.3 0.0 all-reduce.2.cloned.1.call-update
  161.3 0.0 all-gather.13.cloned.1.call-start
  161.3 0.5 all-gather.13.cloned.1.call-update
  161.9 13.4 %all-gather.9.cloned.1.call-done = bf16[256,3072]{1,0:T(8,128)(2,1)} async-done(((bf16[256,1536]{1,0:T(8,128)(2,1)}), bf16[256,3072]{1,0:T(8,128)(2,1)}) %all-gather.9.cloned.1.call-update) | async-done | bytes 1572880 | tf_op jit(solution)/shard_map/all_gather | solution.py:51
  175.3 2.6 copy.13
  177.9 7.3 %all-to-all-start = ((bf16[256,16,192]{0,2,1:T(8,128)(2,1)}), bf16[256,16,192]{0,2,1:T(8,128)(2,1)S(1)}, u32[]{:S(2)}, u32[]{:S(2)}) async-start(bf16[256,16,192]{0,2,1:T(8,128)(2,1)} %bitcast.9), calls=%async_computation | async-start | bytes 3145728 | tf_op jit(solution)/shard_map/all_to_all | solution.py:57
  185.1 0.0 copy-start.1
  185.2 0.0 copy-done
  185.2 0.2 fusion.20
  185.3 96.5 %all-reduce.2.cloned.1.call-done = f32[64,1536]{1,0:T(8,128)} async-done(((f32[64,1536]{1,0:T(8,128)}), f32[64,1536]{1,0:T(8,128)}) %all-reduce.2.cloned.1.call-update) | async-done | bytes 393232 | tf_op jit(solution)/shard_map/psum | solution.py:46
  281.9 1.7 negate_bitcast_fusion.1
  283.6 2.2 all_gather.19
  285.8 0.0 copy-done.1
  285.8 0.9 negate_bitcast_fusion
  286.7 0.0 all-to-all-done
  286.7 0.0 copy-start.6
  286.7 0.2 copy.15
  286.9 53.6 %all-gather.13.cloned.1.call-done = bf16[1,4096,512]{2,1,0:T(8,128)(2,1)} async-done(((bf16[1,256,512]{2,1,0:T(8,128)(2,1)}), bf16[1,4096,512]{2,1,0:T(8,128)(2,1)}) %all-gather.13.cloned.1.call-update) | async-done | bytes 4194320 | tf_op jit(solution)/shard_map/all_gather | solution.py:58
  340.5 0.0 copy-done.6
  340.5 0.0 copy-start.5
  340.5 8.4 %fusion.5 = f32[192,2048]{1,0:T(8,128)S(1)} fusion(bf16[4096,192]{0,1:T(8,128)(2,1)S(1)} %bitcast.36, bf16[4096,512]{1,0:T(8,128)(2,1)} %bitcast.39, bf16[4096,1536]{1,0:T(8,128)(2,1)} %bitcast.38, bf16[192,512]{1,0:T(8,128)(2,1)S(1)} %bitcast.42, bf16[192,1536]{1,0:T(8,128)(2,1)} %bitcast.41), kind=kOutput, calls=%fused_computation.7 | convolution fusion | flops 3256745984 | bytes 20709376 | tf_op jit(solution)/shard_map/dot_general | solution.py:14
  348.9 0.0 copy-done.5
  348.9 1.3 fusion.8
  350.2 0.9 slice_bitcast_fusion
  351.0 0.7 slice_bitcast_fusion.1
Async XLA Ops:
  7.2 178.0 %copy-start = (bf16[64,64]{1,0:T(8,128)(2,1)S(1)}, bf16[64,64]{1,0:T(8,128)(2,1)}, u32[]{:S(2)}) copy-start(bf16[64,64]{1,0:T(8,128)(2,1)} %param.15) | copy-start | bytes 24580
  7.2 30.3 %copy-start.7 = (bf16[1,64,256]{2,1,0:T(8,128)(2,1)S(1)}, bf16[1,64,256]{2,1,0:T(8,128)(2,1)}, u32[]{:S(2)}) copy-start(bf16[1,64,256]{2,1,0:T(8,128)(2,1)} %param.10) | copy-start | bytes 98308
  7.2 45.9 %all-gather.7.cloned.1.call-start = ((), (), s32[]{:S(2)}) async-start(), calls=%async_computation.1 | async-start | bytes 3145728 | tf_op jit(solution)/shard_map/all_gather | solution.py:40
  7.2 28.4 %collective-permute-start.1 = (bf16[256,2048]{1,0:T(8,128)(2,1)}, bf16[256,2048]{1,0:T(8,128)(2,1)S(1)}, u32[]{:S(2)}, u32[]{:S(2)}) collective-permute-start(bf16[256,2048]{1,0:T(8,128)(2,1)} %bitcast.40), channel_id=1, source_target_pairs={{32,0},{64,32},{96,64},{128,96},{160,128},{192,160},{224,192},{33,... | collective-permute-start | bytes 3145736 | tf_op jit(solution)/shard_map/ppermute | solution.py:10
  35.6 1.0 copy-start.4
  36.7 115.2 %all-gather.11.cloned.1.call-start = ((), (), s32[]{:S(2)}) async-start(), calls=%async_computation.4 | async-start | bytes 13369344 | tf_op jit(solution)/shard_map/all_gather | solution.py:36
  37.4 137.9 %all-gather.9.cloned.1.call-start = ((), (), s32[]{:S(2)}) async-start(), calls=%async_computation.3 | async-start | bytes 2359296 | tf_op jit(solution)/shard_map/all_gather | solution.py:51
  37.5 121.4 %copy-start.3 = (bf16[1,64,1536]{2,1,0:T(8,128)(2,1)S(1)}, bf16[1,64,1536]{2,1,0:T(8,128)(2,1)}, u32[]{:S(2)}) copy-start(bf16[1,64,1536]{2,1,0:T(8,128)(2,1)} %param.13) | copy-start | bytes 589828
  37.5 121.4 %collective-permute-start = (bf16[64,256]{1,0:T(8,128)(2,1)S(1)}, bf16[64,256]{1,0:T(8,128)(2,1)S(1)}, u32[]{:S(2)}, u32[]{:S(2)}) collective-permute-start(bf16[64,256]{1,0:T(8,128)(2,1)S(1)} %bitcast.43), channel_id=1, source_target_pairs={{32,0},{64,32},{96,64},{128,96},{160,128},{192,160},{224,192},{33,... | collective-permute-start | bytes 98312 | tf_op jit(solution)/shard_map/ppermute | solution.py:10
  158.9 1.4 copy-start.2
  160.2 121.7 %all-reduce.2.cloned.1.call-start = ((), (), s32[]{:S(2)}) async-start(), calls=%async_computation.2 | async-start | bytes 786432 | tf_op jit(solution)/shard_map/psum | solution.py:46
  161.3 179.2 %all-gather.13.cloned.1.call-start = ((), (), s32[]{:S(2)}) async-start(), calls=%async_computation.5 | async-start | bytes 4456448 | tf_op jit(solution)/shard_map/all_gather | solution.py:58
  177.9 108.9 %all-to-all-start = ((bf16[256,16,192]{0,2,1:T(8,128)(2,1)}), bf16[256,16,192]{0,2,1:T(8,128)(2,1)S(1)}, u32[]{:S(2)}, u32[]{:S(2)}) async-start(bf16[256,16,192]{0,2,1:T(8,128)(2,1)} %bitcast.9), calls=%async_computation | async-start | bytes 3145728 | tf_op jit(solution)/shard_map/all_to_all | solution.py:57
  185.1 100.7 %copy-start.1 = (bf16[256,1536]{1,0:T(8,128)(2,1)S(1)}, bf16[256,1536]{1,0:T(8,128)(2,1)}, u32[]{:S(2)}) copy-start(bf16[256,1536]{1,0:T(8,128)(2,1)} %fusion.4) | copy-start | bytes 2359300
  286.7 53.8 %copy-start.6 = (bf16[1,192,512]{2,1,0:T(8,128)(2,1)S(1)}, bf16[1,192,512]{2,1,0:T(8,128)(2,1)}, u32[]{:S(2)}) copy-start(bf16[1,192,512]{2,1,0:T(8,128)(2,1)} %param.17) | copy-start | bytes 589828
  340.5 8.4 %copy-start.5 = (bf16[1,64,512]{2,1,0:T(8,128)(2,1)S(1)}, bf16[1,64,512]{2,1,0:T(8,128)(2,1)}, u32[]{:S(2)}) copy-start(bf16[1,64,512]{2,1,0:T(8,128)(2,1)} %param.14) | copy-start | bytes 196612
Sparse Core Ops, SparseCore 0:
  36.8 16.2 all-gather.6
  55.6 96.2 all-gather.10
  160.3 14.9 all-gather.8
  178.9 102.8 all-reduce.1
  284.2 56.2 all-gather.12
where the time goes:
time: 361 us; the launch traced here: 358 us
  waiting for transfers between devices  303 us (84%)
  matrix products  19.1 us (5%)
  between operations  13.9 us (4%)
  starting transfers between devices  11.5 us (3%)
  local copies, waits for them, and re-layouts  5.35 us (1%)
    all_gather x1, waiting for transfers between devices, per_device(): factor_column = lax.all_gather(factor_tile, 'row', axis=0, tiled=True)  98.7 us
    psum x1, waiting for transfers between devices, per_device(): lax.psum(y_part, 'row')  96.5 us
    all_gather x1, waiting for transfers between devices, per_device(): rest_column = lax.all_gather(factor_other, 'row', axis=0, tiled=True)  53.6 us
    ppermute x2, waiting for transfers between devices, shifted(): lax.ppermute(value, axis, [(source, source + steps) for source in range(l...  26.4 us
    all_gather x1, waiting for transfers between devices, per_device(): lax.all_gather(inverse_next, 'col', axis=1, tiled=True)  13.6 us
    all_gather x1, waiting for transfers between devices, per_device(): lax.all_gather(x_bf, 'col', axis=1, tiled=True)  13.4 us
    dot_general x3, matrix products, contract_first(): lax.dot_general(left, right, (((0,), (0,)), ((), ())), preferred_element_...  10.9 us
    all_to_all x1, starting transfers between devices, per_device(): lax.all_to_all(x_panel, 'row', split_axis=1, concat_axis=0, tiled=True)  7.26 us
  transfers between devices with their start and end apart: 8, of which 6 were waited for; matrix products, arithmetic and copies ran while one was open for 4% of the time, Pallas kernels for 0%

commit v1 on v0

v1 whole, which is shorter than its diff:
```python
import jax
import jax.numpy as jnp
from jax import lax
from jax.experimental import pallas as pl
from jax.experimental.pallas import tpu as pltpu
from jax.sharding import PartitionSpec as P

MESH = pl.DeviceIdType.MESH
BF16 = jnp.bfloat16
F32 = jnp.float32

BLOCK = 256
WIN = 1536
REST = 512
FULL = WIN + REST
ARROW = 64
DROWS = 192
TOP = 144
PIECE = 272
S_CHUNKS = 4
S_ROWS = BLOCK // S_CHUNKS
TILE = 256


def dot(left, right):
    return jnp.dot(left, right, preferred_element_type=F32)


def al(value, multiple):
    return pl.multiple_of(value, multiple)


def kernel(
    s_in, r_in, fw_in, fr_in, aw_in, ar_in, tip_in, bw_in, br_in,
    x_out, y_out, dw_out, dr_out,
    sz, rz, sg, fg, av, tip, base,
    x_send, x_hold, x_relay, x_recv, x_own, x_neg, xt, xg,
    y_all, yt, y_neg,
    d_send, d_hold, d_relay, d_recv, d_own, dw, dr,
    loc_sem, z_send, z_recv, f_send, f_recv, r_send, r_recv, sa_send, sa_recv,
    xr_send, xr_recv, xa_send, xa_recv, y_send, y_recv, t_send, t_recv,
    dr_send, dr_recv, out_sem,
):
    z = lax.axis_index("dom")
    row = lax.axis_index("row")
    k = lax.axis_index("col")
    y = row // 4
    x = row % 4
    a = (1 - k) * y + k * x
    b = (1 - k) * x + k * y
    stride_a = 4 - 3 * k
    stride_b = 1 + 3 * k

    def at(a_pos, b_pos):
        return {"row": a_pos * stride_a + b_pos * stride_b, "col": k}

    a_next, a_prev = (a + 1) % 4, (a + 3) % 4
    b_next, b_prev, b_opp = (b + 1) % 4, (b + 3) % 4, (b + 2) % 4

    pending = []

    def remote(src, dst, send_sem, recv_sem, device):
        copy = pltpu.make_async_remote_copy(
            src_ref=src, dst_ref=dst, send_sem=send_sem, recv_sem=recv_sem,
            device_id=device, device_id_type=MESH,
        )
        copy.start()
        pending.append((copy, None))
        return copy

    def remote_or_local(src, dst, send_sem, recv_sem, device, here, keep=True):
        copy = pltpu.make_async_remote_copy(
            src_ref=src, dst_ref=dst, send_sem=send_sem, recv_sem=recv_sem,
            device_id=device, device_id_type=MESH,
        )

        @pl.when(here)
        def _():
            pltpu.make_async_copy(src, dst, recv_sem).start()

        @pl.when(jnp.logical_not(here))
        def _():
            copy.start()

        if keep:
            pending.append((copy, here))

    def arrived(ref, sem):
        pltpu.make_async_copy(ref, ref, sem).wait()

    barrier = pltpu.get_barrier_semaphore()
    greeted = 0
    for step in (1, 7):
        pl.semaphore_signal(barrier, inc=1, device_id={"dom": (z + step) % 8}, device_id_type=MESH)
        greeted += 1
    pl.semaphore_signal(barrier, inc=1, device_id={"col": 1 - k}, device_id_type=MESH)
    greeted += 1
    for step in (1, 2, 3):
        for core in (0, 1):
            pl.semaphore_signal(
                barrier, inc=1, device_id={"row": y * 4 + (x + step) % 4, "col": core}, device_id_type=MESH
            )
            pl.semaphore_signal(
                barrier, inc=1, device_id={"row": ((y + step) % 4) * 4 + x, "col": core}, device_id_type=MESH
            )
            greeted += 2

    own_rows = pl.ds(al(a * BLOCK, BLOCK), BLOCK)
    locals_ = [
        pltpu.make_async_copy(fw_in, fg.at[own_rows, pl.ds(0, WIN)], loc_sem.at[0]),
        pltpu.make_async_copy(fr_in, fg.at[own_rows, pl.ds(WIN, REST)], loc_sem.at[1]),
        pltpu.make_async_copy(aw_in, av.at[:, pl.ds(0, WIN)], loc_sem.at[2]),
        pltpu.make_async_copy(ar_in, av.at[:, pl.ds(WIN, REST)], loc_sem.at[3]),
        pltpu.make_async_copy(tip_in, tip, loc_sem.at[4]),
        pltpu.make_async_copy(bw_in, base.at[:, pl.ds(0, WIN)], loc_sem.at[5]),
        pltpu.make_async_copy(br_in, base.at[:, pl.ds(WIN, REST)], loc_sem.at[6]),
    ]
    for copy in locals_:
        copy.start()

    pl.semaphore_wait(barrier, greeted)

    below = {"dom": (z + 7) % 8}
    z_copies = [remote(r_in, rz, z_send.at[S_CHUNKS], z_recv.at[S_CHUNKS], below)]
    for chunk in range(S_CHUNKS):
        rows = pl.ds(chunk * S_ROWS, S_ROWS)
        z_copies.append(remote(s_in.at[rows, :], sz.at[rows, :], z_send.at[chunk], z_recv.at[chunk], below))

    half = BLOCK // 2

    def block_half(a_pos, part, first, count):
        return fg.at[pl.ds(al(a_pos * BLOCK + part * half, half), half), pl.ds(first, count)]

    def f_own(source, first, count, base_sem):
        for part in (0, 1):
            src = source.at[pl.ds(part * half, half), :]
            remote(src, block_half(a, part, first, count), f_send.at[base_sem + part],
                   f_recv.at[base_sem + part], at(a_next, b))
            src = source.at[pl.ds((1 - part) * half, half), :]
            remote(src, block_half(a, 1 - part, first, count), f_send.at[base_sem + 3 - part],
                   f_recv.at[base_sem + 3 - part], at(a_prev, b))

    def f_forward(first, count, base_sem):
        block = block_half(a_prev, 0, first, count)
        arrived(block, f_recv.at[base_sem])
        remote(block, block, f_send.at[base_sem + 4], f_recv.at[base_sem + 4], at(a_next, b))
        block = block_half(a_next, 1, first, count)
        arrived(block, f_recv.at[base_sem + 3])
        remote(block, block, f_send.at[base_sem + 5], f_recv.at[base_sem + 5], at(a_prev, b))

    def f_rest_of(first, count, base_sem):
        arrived(block_half(a_prev, 1, first, count), f_recv.at[base_sem + 1])
        arrived(block_half(a_next, 0, first, count), f_recv.at[base_sem + 2])
        far = (a + 2) % 4
        arrived(block_half(far, 0, first, count), f_recv.at[base_sem + 4])
        arrived(block_half(far, 1, first, count), f_recv.at[base_sem + 5])

    f_own(fw_in, 0, WIN, 0)

    arrived(rz, z_recv.at[S_CHUNKS])

    @pl.when(z == 7)
    def _():
        rz[...] = jnp.zeros_like(rz)

    r_dst = sg.at[:, pl.ds(128, 16), pl.ds(al(a * BLOCK, BLOCK), BLOCK)]
    for step in (1, 2, 3):
        remote(rz, r_dst, r_send.at[step - 1], r_recv, at((a + step) % 4, b))
    pltpu.make_async_copy(rz, r_dst, r_recv).start()

    def s_spread(chunk):
        first = chunk * S_ROWS
        rows = pl.ds(first, S_ROWS)
        into = pl.ds(first + 16 * (first // 128), S_ROWS)
        arrived(sz.at[rows, :], z_recv.at[chunk])

        @pl.when(z == 7)
        def _():
            sz[rows, :] = jnp.zeros((S_ROWS, 2048), BF16)

        index = 0
        for step in range(4):
            x_to = (x + step) % 4
            for part in range(2):
                src = sz.at[rows, pl.ds(al((part * 4 + x_to) * BLOCK, BLOCK), BLOCK)]
                dst = sg.at[x, into, pl.ds(al((2 * k + part) * BLOCK, BLOCK), BLOCK)]
                device = {"row": y * 4 + x_to, "col": 0}
                sems = (sa_send.at[chunk, index], sa_recv.at[x], device)
                if step:
                    remote(src, dst, *sems)
                else:
                    remote_or_local(src, dst, *sems, k == 0)
                index += 1
        for part in range(2):
            y_to = 2 * k + part
            src = sz.at[rows, pl.ds(part * 1024, 1024)]
            dst = sg.at[y, into, :]
            device = {"row": y_to * 4 + x, "col": 1}
            here = jnp.logical_and(y_to == y, k == 1)
            remote_or_local(src, dst, sa_send.at[chunk, index], sa_recv.at[y], device, here)
            index += 1

    s_spread(0)
    f_forward(0, WIN, 0)
    s_spread(1)
    s_spread(2)
    f_own(fr_in, WIN, REST, 6)
    s_spread(3)
    f_forward(WIN, REST, 6)

    for copy in locals_:
        copy.wait()
    f_rest_of(0, WIN, 0)
    arrived(sg.at[:, pl.ds(128, 16), :], r_recv)

    def reduce_scatter(chunks, width, top, piece, product, send, hold, relay, recv, s_sem, r_sem, ready):
        def part_of(ref, lead, upper, cols):
            rows = pl.ds(0, top) if upper else pl.ds(top, piece - top)
            return ref.at[lead, rows, cols] if lead is not None else ref.at[rows, cols]

        def opposite(c):
            def body(n, _):
                cols = pl.ds(al(c * width + n * TILE, TILE), TILE)
                send[0, :, cols] = product(b_opp, cols).astype(BF16)
                return 0

            lax.fori_loop(0, width // TILE, body, 0)
            cols = pl.ds(c * width, width)
            remote(part_of(send, 0, True, cols), part_of(relay, None, True, cols),
                   s_sem.at[c, 0], r_sem.at[c, 0], at(a, b_next))
            remote(part_of(send, 0, False, cols), part_of(relay, None, False, cols),
                   s_sem.at[c, 1], r_sem.at[c, 1], at(a, b_prev))

        def beside(c):
            def body_next(n, _):
                cols = pl.ds(al(c * width + n * TILE, TILE), TILE)
                value = product(b_next, cols)
                hold[pl.ds(0, top), cols] = value[:top]
                send[1, pl.ds(top, piece - top), cols] = value[top:].astype(BF16)
                return 0

            def body_prev(n, _):
                cols = pl.ds(al(c * width + n * TILE, TILE), TILE)
                value = product(b_prev, cols)
                hold[pl.ds(top, piece - top), cols] = value[top:]
                send[2, pl.ds(0, top), cols] = value[:top].astype(BF16)
                return 0

            cols = pl.ds(c * width, width)
            lax.fori_loop(0, width // TILE, body_next, 0)
            remote(part_of(send, 1, False, cols), part_of(recv, 0, False, cols),
                   s_sem.at[c, 2], r_sem.at[c, 2], at(a, b_next))
            lax.fori_loop(0, width // TILE, body_prev, 0)
            remote(part_of(send, 2, True, cols), part_of(recv, 1, True, cols),
                   s_sem.at[c, 3], r_sem.at[c, 3], at(a, b_prev))

        def relayed(c):
            cols = pl.ds(c * width, width)
            arrived(part_of(relay, None, True, cols), r_sem.at[c, 0])
            rows = pl.ds(0, top)
            send[1, rows, cols] = (hold[rows, cols] + relay[rows, cols].astype(F32)).astype(BF16)
            remote(part_of(send, 1, True, cols), part_of(recv, 0, True, cols),
                   s_sem.at[c, 4], r_sem.at[c, 4], at(a, b_next))
            arrived(part_of(relay, None, False, cols), r_sem.at[c, 1])
            rows = pl.ds(top, piece - top)
            send[2, rows, cols] = (hold[rows, cols] + relay[rows, cols].astype(F32)).astype(BF16)
            remote(part_of(send, 2, False, cols), part_of(recv, 1, False, cols),
                   s_sem.at[c, 5], r_sem.at[c, 5], at(a, b_prev))

        def received(c):
            cols = pl.ds(c * width, width)
            arrived(part_of(recv, 0, False, cols), r_sem.at[c, 2])
            arrived(part_of(recv, 1, True, cols), r_sem.at[c, 3])
            arrived(part_of(recv, 0, True, cols), r_sem.at[c, 4])
            arrived(part_of(recv, 1, False, cols), r_sem.at[c, 5])

        return opposite, beside, relayed, received

    def x_product(b_pos, cols):
        return dot(sg[b_pos], fg[:, cols])

    x_width = 768
    opposite, beside, relayed, received = reduce_scatter(
        2, x_width, TOP, PIECE, x_product, x_send, x_hold, x_relay, x_recv, xr_send, xr_recv, None
    )

    def x_here(c):
        def body(n, _):
            cols = pl.ds(al(c * x_width + n * TILE, TILE), TILE)
            value = x_product(b, cols)
            arrow = lax.dot_general(
                rz[...].reshape(ARROW, BLOCK), av[:, cols], (((0,), (0,)), ((), ())),
                preferred_element_type=F32,
            )
            mine = tip[pl.ds(al(b * 16, 16), 16), :]
            x_own[pl.ds(0, 128), cols] = value[:128] + arrow[:128]
            x_own[pl.ds(128, 16), cols] = value[128:TOP] + dot(mine, av[:, cols])
            x_own[pl.ds(TOP, 128), cols] = value[TOP:] + arrow[128:]
            return 0

        lax.fori_loop(0, x_width // TILE, body, 0)

    y_rows = pl.ds(al(b * 16, 16), 16)

    def x_final(c):
        received(c)

        def body(n, _):
            cols = pl.ds(al(c * x_width + n * TILE, TILE), TILE)
            total = x_own[:, cols] + x_recv[0, :, cols].astype(F32) + x_recv[1, :, cols].astype(F32)
            top = total[:128].astype(BF16)
            bottom = total[TOP:].astype(BF16)
            x_neg[pl.ds(0, 128), cols] = -top
            x_neg[pl.ds(128, 128), cols] = -bottom
            xt[cols, pl.ds(0, 128)] = top.T
            xt[cols, pl.ds(128, 128)] = bottom.T
            y_all[k, y_rows, cols] = total[128:TOP].astype(BF16)
            return 0

        lax.fori_loop(0, x_width // TILE, body, 0)
        y_to = 2 * k + c
        here = jnp.logical_and(y_to == y, k == 0)
        remote_or_local(
            xt.at[pl.ds(c * 768, 768), :], xg.at[:, pl.ds(al(y * BLOCK, BLOCK), BLOCK)],
            xa_send.at[c, 0], xa_recv.at[y], {"row": y_to * 4 + x, "col": 0}, here,
        )
        for step in range(4):
            x_to = (x + step) % 4
            src = xt.at[pl.ds(al(c * 768 + x_to * DROWS, 64), DROWS), :]
            dst = xg.at[pl.ds(al(y_to * DROWS, 64), DROWS), pl.ds(al(x * BLOCK, BLOCK), BLOCK)]
            sems = (xa_send.at[c, 1 + step], xa_recv.at[x], {"row": y * 4 + x_to, "col": 1})
            if step:
                remote(src, dst, *sems)
            else:
                remote_or_local(src, dst, *sems, k == 1)

    arrived(sg.at[b_opp, pl.ds(0, BLOCK), :], sa_recv.at[b_opp])
    opposite(0)
    arrived(sg.at[b_next, pl.ds(0, BLOCK), :], sa_recv.at[b_next])
    arrived(sg.at[b_prev, pl.ds(0, BLOCK), :], sa_recv.at[b_prev])
    beside(0)
    opposite(1)
    relayed(0)
    beside(1)
    arrived(sg.at[b, pl.ds(0, BLOCK), :], sa_recv.at[b])
    x_here(0)
    relayed(1)
    x_here(1)
    x_final(0)
    x_final(1)
    outs = [pltpu.make_async_copy(x_neg, x_out, out_sem.at[0])]
    outs[0].start()

    y_mine = y_all.at[k, y_rows, :]
    for step in (1, 2, 3):
        remote(y_mine, y_mine, y_send.at[step - 1], y_recv.at[step - 1], at(a, (b + step) % 4))

    f_rest_of(WIN, REST, 6)
    for a_pos in range(4):
        arrived(xg.at[:, pl.ds(a_pos * BLOCK, BLOCK)], xa_recv.at[a_pos])

    def d_product(b_pos, cols):
        return dot(xg[pl.ds(al(b_pos * DROWS, 64), DROWS), :], fg[:, cols])

    d_width = 1024
    opposite, beside, relayed, received = reduce_scatter(
        2, d_width, DROWS // 2, DROWS, d_product, d_send, d_hold, d_relay, d_recv, dr_send, dr_recv, None
    )
    opposite(0)
    beside(0)
    opposite(1)
    for step in (1, 2, 3):
        theirs = y_all.at[k, pl.ds(al(((b + 4 - step) % 4) * 16, 16), 16), :]
        arrived(theirs, y_recv.at[step - 1])
    remote(y_all.at[k], y_all.at[k], t_send, t_recv, {"col": 1 - k})
    relayed(0)
    beside(1)
    y_neg[...] = -y_all[k]
    outs.append(pltpu.make_async_copy(y_neg, y_out, out_sem.at[1]))
    outs[1].start()
    arrived(y_all.at[1 - k], t_recv)
    yt[...] = y_all[row // 8].T

    def d_here(c):
        def body(n, _):
            cols = pl.ds(al(c * d_width + n * TILE, TILE), TILE)
            value = d_product(b, cols)
            mine = yt[pl.ds(al((row % 8) * DROWS, 64), DROWS), :]
            d_own[:, cols] = value + base[:, cols].astype(F32) + dot(mine, av[:, cols])
            return 0

        lax.fori_loop(0, d_width // TILE, body, 0)

    d_here(0)
    relayed(1)
    d_here(1)

    received(0)
    cols = pl.ds(0, d_width)
    dw[:, cols] = (d_own[:, cols] + d_recv[0, :, cols].astype(F32) + d_recv[1, :, cols].astype(F32)).astype(BF16)
    received(1)
    cols = pl.ds(d_width, WIN - d_width)
    dw[:, cols] = (d_own[:, cols] + d_recv[0, :, cols].astype(F32) + d_recv[1, :, cols].astype(F32)).astype(BF16)
    outs.append(pltpu.make_async_copy(dw, dw_out, out_sem.at[2]))
    outs[2].start()
    cols = pl.ds(WIN, REST)
    dr[...] = (d_own[:, cols] + d_recv[0, :, cols].astype(F32) + d_recv[1, :, cols].astype(F32)).astype(BF16)
    outs.append(pltpu.make_async_copy(dr, dr_out, out_sem.at[3]))
    outs[3].start()

    for copy, here in pending:
        if here is None:
            copy.wait_send()
        else:
            pl.when(jnp.logical_not(here))(copy.wait_send)
    for copy in outs:
        copy.wait()


def per_device(s, r, fw, fr, aw, ar, tip, bw, br):
    hbm = pl.BlockSpec(memory_space=pl.ANY)
    vmem = pltpu.VMEM
    dma = pltpu.SemaphoreType.DMA
    outs = pl.pallas_call(
        kernel,
        out_shape=(
            jax.ShapeDtypeStruct((BLOCK, WIN), BF16),
            jax.ShapeDtypeStruct((ARROW, WIN), BF16),
            jax.ShapeDtypeStruct((DROWS, WIN), BF16),
            jax.ShapeDtypeStruct((DROWS, REST), BF16),
        ),
        in_specs=[hbm] * 9,
        out_specs=(hbm,) * 4,
        scratch_shapes=[
            vmem((BLOCK, 2048), BF16),
            vmem((4, 16, BLOCK), BF16),
            vmem((4, PIECE, 1024), BF16),
            vmem((1024, FULL), BF16),
            vmem((ARROW, FULL), BF16),
            vmem((ARROW, ARROW), BF16),
            vmem((DROWS, FULL), BF16),
            vmem((3, PIECE, WIN), BF16),
            vmem((PIECE, WIN), F32),
            vmem((PIECE, WIN), BF16),
            vmem((2, PIECE, WIN), BF16),
            vmem((PIECE, WIN), F32),
            vmem((BLOCK, WIN), BF16),
            vmem((WIN, BLOCK), BF16),
            vmem((768, 1024), BF16),
            vmem((2, ARROW, WIN), BF16),
            vmem((WIN, ARROW), BF16),
            vmem((ARROW, WIN), BF16),
            vmem((3, DROWS, FULL), BF16),
            vmem((DROWS, FULL), F32),
            vmem((DROWS, FULL), BF16),
            vmem((2, DROWS, FULL), BF16),
            vmem((DROWS, FULL), F32),
            vmem((DROWS, WIN), BF16),
            vmem((DROWS, REST), BF16),
            dma((7,)),
            dma((S_CHUNKS + 1,)), dma((S_CHUNKS + 1,)),
            dma((12,)), dma((12,)),
            dma((3,)), dma,
            dma((S_CHUNKS, 10)), dma((4,)),
            dma((2, 6)), dma((2, 6)),
            dma((2, 5)), dma((4,)),
            dma((3,)), dma((3,)),
            dma, dma,
            dma((2, 6)), dma((2, 6)),
            dma((4,)),
        ],
        compiler_params=pltpu.CompilerParams(
            collective_id=0, has_side_effects=True, vmem_limit_bytes=60 << 20
        ),
        cost_estimate=pl.CostEstimate(flops=6_800_000_000, bytes_accessed=8_000_000, transcendentals=0),
    )(s[0], r[0].reshape(4, 16, BLOCK), fw[0], fr[0], aw[0], ar[0], tip, bw[0], br[0])
    return tuple(value[None] for value in outs)


def solution(mesh):
    in_specs = (
        P("dom", "row", "col"),
        P("dom", None, "row"),
        P("dom", "row", "col"),
        P("dom", "row", "col"),
        P("dom", None, "col"),
        P("dom", None, "col"),
        P(),
        P("dom", "row", "col"),
        P("dom", "row", "col"),
    )
    out_specs = (
        P("dom", "row", "col"),
        P("dom", None, "col"),
        P("dom", "row", "col"),
        P("dom", "row", "col"),
    )
    return jax.shard_map(
        per_device, mesh=mesh, in_specs=in_specs, out_specs=out_specs, check_vma=False
    )
```

time: 361 us -> 99.7 us (0.28)
  waiting for transfers between devices: 303 us -> 0 us
  Pallas kernels: 0 us -> 93.5 us
  matrix products: 19.1 us -> 0 us
  between operations: 13.9 us -> 0.66 us
  starting transfers between devices: 11.5 us -> 0 us
    all_gather x4 -> x0, waiting for transfers between devices: 179 us -> none  [the longest x1 98.7 us: per_device(): factor_column = lax.all_gather(factor_tile, 'row', axis=0, tiled=True)]
    psum x1 -> x0, waiting for transfers between devices: 96.5 us -> none  [per_device(): lax.psum(y_part, 'row')]
    pallas_call x0 -> x1, Pallas kernels: none -> 93.5 us  [per_device(): pl.pallas_call(kernel, out_shape=(jax.ShapeDtypeStruct((BLOCK, WIN), BF16...]
    ppermute x2 -> x0, waiting for transfers between devices: 26.4 us -> none  [shifted(): lax.ppermute(value, axis, [(source, source + steps) for source in range(l...]
    dot_general x6 -> x0, matrix products: 19.1 us -> none  [the longest x3 10.9 us: contract_first(): lax.dot_general(left, right, (((0,), (0,)), ((), ())), preferred_element_...]
    all_to_all x1 -> x0, starting transfers between devices: 7.26 us -> none  [per_device(): lax.all_to_all(x_panel, 'row', split_axis=1, concat_axis=0, tiled=True)]
    ppermute x2 -> x0, starting transfers between devices: 4.07 us -> none  [shifted(): lax.ppermute(value, axis, [(source, source + steps) for source in range(l...]
  transfers between devices with their start and end apart: 8 -> 0, of which waited for: 6 -> 0; matrix products, arithmetic and copies ran while one was open for 4% -> 0% of each run, Pallas kernels for 0% -> 0%
where the time goes in v1:
time: 99.7 us; the launch traced here: 98.8 us
  Pallas kernels  93.5 us (94%)
  local copies, waits for them, and re-layouts  4.61 us (5%)
    pallas_call x1, Pallas kernels, per_device(): pl.pallas_call(kernel, out_shape=(jax.ShapeDtypeStruct((BLOCK, WIN), BF16...  93.5 us
    unnamed x10, local copies, waits for them, and re-layouts  4.61 us

profile of v1, /device:TPU:104, one launch (start us, length us, event | category | flops | bytes accessed | tf_op | source)
XLA Modules:
  0.0 98.8 jit_solution(14279533937946575266)
XLA Ops:
  0.6 93.5 %shard_map.120 = (bf16[256,1536]{1,0:T(8,128)(2,1)}, bf16[64,1536]{1,0:T(8,128)(2,1)}, bf16[192,1536]{1,0:T(8,128)(2,1)}, bf16[192,512]{1,0:T(8,128)(2,1)}) custom-call(bf16[256,2048]{1,0:T(8,128)(2,1)} %bitcast.16, bf16[4,16,256]{2,1,0:T(8,128)(2,1)} %bitcast.23, bf16[256,1536]{1,0:T(8,128)(2,1)} %bitcast.17, bf16[256,512]{1,0:T(8,128)(2,1)} %bitcast.19, ...), custom_call_target="tpu_custom_call" | custom-call | flops 6800000000 | bytes 8000000 | tf_op jit(solution)/shard_map/pallas_call | solution.py:424
  94.1 0.0 copy-start.2
  94.2 0.0 copy-start
  94.2 2.1 %copy.17 = bf16[1,256,1536]{2,1,0:T(8,128)(2,1)} copy(bf16[1,256,1536]{2,1,0:T(8,128)(2,1)} %bitcast.12) | data formatting | bytes 1572864
  96.3 0.0 copy-done.2
  96.3 0.7 copy.18
  97.0 0.0 copy-done
  97.0 0.0 copy-start.1
  97.0 0.8 copy.19
  97.8 0.3 copy-done.1
  98.1 0.7 copy.20
Async XLA Ops:
  94.1 2.2 %copy-start.2 = (bf16[64,1536]{1,0:T(8,128)(2,1)S(1)}, bf16[64,1536]{1,0:T(8,128)(2,1)}, u32[]{:S(2)}) copy-start(bf16[64,1536]{1,0:T(8,128)(2,1)} %get-tuple-element.9) | copy-start | bytes 589828
  94.2 2.8 %copy-start = (bf16[192,1536]{1,0:T(8,128)(2,1)S(1)}, bf16[192,1536]{1,0:T(8,128)(2,1)}, u32[]{:S(2)}) copy-start(bf16[192,1536]{1,0:T(8,128)(2,1)} %get-tuple-element.10) | copy-start | bytes 1769476
  97.0 1.1 %copy-start.1 = (bf16[192,512]{1,0:T(8,128)(2,1)S(1)}, bf16[192,512]{1,0:T(8,128)(2,1)}, u32[]{:S(2)}) copy-start(bf16[192,512]{1,0:T(8,128)(2,1)} %get-tuple-element.11) | copy-start | bytes 589828

commit v2 on v1

--- a/solution.py
+++ b/solution.py
@@ -121,10 +121,15 @@
     pl.semaphore_wait(barrier, greeted)
 
     below = {"dom": (z + 7) % 8}
-    z_copies = [remote(r_in, rz, z_send.at[S_CHUNKS], z_recv.at[S_CHUNKS], below)]
-    for chunk in range(S_CHUNKS):
+    remote(r_in, rz, z_send.at[S_CHUNKS], z_recv.at[S_CHUNKS], below)
+    z_copies = []
+
+    def z_start(chunk):
         rows = pl.ds(chunk * S_ROWS, S_ROWS)
         z_copies.append(remote(s_in.at[rows, :], sz.at[rows, :], z_send.at[chunk], z_recv.at[chunk], below))
+
+    z_start(0)
+    z_start(1)
 
     half = BLOCK // 2
 
@@ -173,6 +178,10 @@
         rows = pl.ds(first, S_ROWS)
         into = pl.ds(first + 16 * (first // 128), S_ROWS)
         arrived(sz.at[rows, :], z_recv.at[chunk])
+        if chunk + 2 < S_CHUNKS:
+            z_copies[chunk].wait_send()
+            pending[:] = [item for item in pending if item[0] is not z_copies[chunk]]
+            z_start(chunk + 2)
 
         @pl.when(z == 7)
         def _():
@@ -204,58 +213,45 @@
     f_forward(0, WIN, 0)
     s_spread(1)
     s_spread(2)
+    s_spread(3)
     f_own(fr_in, WIN, REST, 6)
-    s_spread(3)
-    f_forward(WIN, REST, 6)
 
     for copy in locals_:
         copy.wait()
     f_rest_of(0, WIN, 0)
     arrived(sg.at[:, pl.ds(128, 16), :], r_recv)
 
-    def reduce_scatter(chunks, width, top, piece, product, send, hold, relay, recv, s_sem, r_sem, ready):
+    def reduce_scatter(width, turn, top, piece, product, send, hold, relay, recv, s_sem, r_sem):
+        def first_of(c):
+            return al((c + turn) % 2 * width, TILE)
+
         def part_of(ref, lead, upper, cols):
             rows = pl.ds(0, top) if upper else pl.ds(top, piece - top)
             return ref.at[lead, rows, cols] if lead is not None else ref.at[rows, cols]
 
         def opposite(c):
-            def body(n, _):
-                cols = pl.ds(al(c * width + n * TILE, TILE), TILE)
-                send[0, :, cols] = product(b_opp, cols).astype(BF16)
-                return 0
-
-            lax.fori_loop(0, width // TILE, body, 0)
-            cols = pl.ds(c * width, width)
+            cols = pl.ds(first_of(c), width)
+            send[0, :, cols] = product(b_opp, cols).astype(BF16)
             remote(part_of(send, 0, True, cols), part_of(relay, None, True, cols),
                    s_sem.at[c, 0], r_sem.at[c, 0], at(a, b_next))
             remote(part_of(send, 0, False, cols), part_of(relay, None, False, cols),
                    s_sem.at[c, 1], r_sem.at[c, 1], at(a, b_prev))
 
         def beside(c):
-            def body_next(n, _):
-                cols = pl.ds(al(c * width + n * TILE, TILE), TILE)
-                value = product(b_next, cols)
-                hold[pl.ds(0, top), cols] = value[:top]
-                send[1, pl.ds(top, piece - top), cols] = value[top:].astype(BF16)
-                return 0
-
-            def body_prev(n, _):
-                cols = pl.ds(al(c * width + n * TILE, TILE), TILE)
-                value = product(b_prev, cols)
-                hold[pl.ds(top, piece - top), cols] = value[top:]
-                send[2, pl.ds(0, top), cols] = value[:top].astype(BF16)
-                return 0
-
-            cols = pl.ds(c * width, width)
-            lax.fori_loop(0, width // TILE, body_next, 0)
+            cols = pl.ds(first_of(c), width)
+            value = product(b_next, cols)
+            hold[pl.ds(0, top), cols] = value[:top]
+            send[1, pl.ds(top, piece - top), cols] = value[top:].astype(BF16)
             remote(part_of(send, 1, False, cols), part_of(recv, 0, False, cols),
                    s_sem.at[c, 2], r_sem.at[c, 2], at(a, b_next))
-            lax.fori_loop(0, width // TILE, body_prev, 0)
+            value = product(b_prev, cols)
+            hold[pl.ds(top, piece - top), cols] = value[top:]
+            send[2, pl.ds(0, top), cols] = value[:top].astype(BF16)
             remote(part_of(send, 2, True, cols), part_of(recv, 1, True, cols),
                    s_sem.at[c, 3], r_sem.at[c, 3], at(a, b_prev))
 
         def relayed(c):
-            cols = pl.ds(c * width, width)
+            cols = pl.ds(first_of(c), width)
             arrived(part_of(relay, None, True, cols), r_sem.at[c, 0])
             rows = pl.ds(0, top)
             send[1, rows, cols] = (hold[rows, cols] + relay[rows, cols].astype(F32)).astype(BF16)
@@ -268,7 +264,7 @@
                    s_sem.at[c, 5], r_sem.at[c, 5], at(a, b_prev))
 
         def received(c):
-            cols = pl.ds(c * width, width)
+            cols = pl.ds(first_of(c), width)
             arrived(part_of(recv, 0, False, cols), r_sem.at[c, 2])
             arrived(part_of(recv, 1, True, cols), r_sem.at[c, 3])
             arrived(part_of(recv, 0, True, cols), r_sem.at[c, 4])
@@ -281,32 +277,30 @@
 
     x_width = 768
     opposite, beside, relayed, received = reduce_scatter(
-        2, x_width, TOP, PIECE, x_product, x_send, x_hold, x_relay, x_recv, xr_send, xr_recv, None
+        x_width, a, TOP, PIECE, x_product, x_send, x_hold, x_relay, x_recv, xr_send, xr_recv
     )
 
     def x_here(c):
-        def body(n, _):
-            cols = pl.ds(al(c * x_width + n * TILE, TILE), TILE)
-            value = x_product(b, cols)
-            arrow = lax.dot_general(
-                rz[...].reshape(ARROW, BLOCK), av[:, cols], (((0,), (0,)), ((), ())),
-                preferred_element_type=F32,
-            )
-            mine = tip[pl.ds(al(b * 16, 16), 16), :]
-            x_own[pl.ds(0, 128), cols] = value[:128] + arrow[:128]
-            x_own[pl.ds(128, 16), cols] = value[128:TOP] + dot(mine, av[:, cols])
-            x_own[pl.ds(TOP, 128), cols] = value[TOP:] + arrow[128:]
-            return 0
-
-        lax.fori_loop(0, x_width // TILE, body, 0)
+        cols = pl.ds(al((c + a) % 2 * x_width, TILE), x_width)
+        value = x_product(b, cols)
+        arrow = lax.dot_general(
+            rz[...].reshape(ARROW, BLOCK), av[:, cols], (((0,), (0,)), ((), ())),
+            preferred_element_type=F32,
+        )
+        mine = tip[pl.ds(al(b * 16, 16), 16), :]
+        x_own[pl.ds(0, 128), cols] = value[:128] + arrow[:128]
+        x_own[pl.ds(128, 16), cols] = value[128:TOP] + dot(mine, av[:, cols])
+        x_own[pl.ds(TOP, 128), cols] = value[TOP:] + arrow[128:]
 
     y_rows = pl.ds(al(b * 16, 16), 16)
 
     def x_final(c):
         received(c)
+        turn = (c + a) % 2
+        first = turn * x_width
 
         def body(n, _):
-            cols = pl.ds(al(c * x_width + n * TILE, TILE), TILE)
+            cols = pl.ds(al(first + n * TILE, TILE), TILE)
             total = x_own[:, cols] + x_recv[0, :, cols].astype(F32) + x_recv[1, :, cols].astype(F32)
             top = total[:128].astype(BF16)
             bottom = total[TOP:].astype(BF16)
@@ -318,15 +312,15 @@
             return 0
 
         lax.fori_loop(0, x_width // TILE, body, 0)
-        y_to = 2 * k + c
+        y_to = 2 * k + turn
         here = jnp.logical_and(y_to == y, k == 0)
         remote_or_local(
-            xt.at[pl.ds(c * 768, 768), :], xg.at[:, pl.ds(al(y * BLOCK, BLOCK), BLOCK)],
+            xt.at[pl.ds(al(first, TILE), x_width), :], xg.at[:, pl.ds(al(y * BLOCK, BLOCK), BLOCK)],
             xa_send.at[c, 0], xa_recv.at[y], {"row": y_to * 4 + x, "col": 0}, here,
         )
         for step in range(4):
             x_to = (x + step) % 4
-            src = xt.at[pl.ds(al(c * 768 + x_to * DROWS, 64), DROWS), :]
+            src = xt.at[pl.ds(al(first + x_to * DROWS, 64), DROWS), :]
             dst = xg.at[pl.ds(al(y_to * DROWS, 64), DROWS), pl.ds(al(x * BLOCK, BLOCK), BLOCK)]
             sems = (xa_send.at[c, 1 + step], xa_recv.at[x], {"row": y * 4 + x_to, "col": 1})
             if step:
@@ -340,6 +334,7 @@
     arrived(sg.at[b_prev, pl.ds(0, BLOCK), :], sa_recv.at[b_prev])
     beside(0)
     opposite(1)
+    f_forward(WIN, REST, 6)
     relayed(0)
     beside(1)
     arrived(sg.at[b, pl.ds(0, BLOCK), :], sa_recv.at[b])
@@ -364,7 +359,7 @@
 
     d_width = 1024
     opposite, beside, relayed, received = reduce_scatter(
-        2, d_width, DROWS // 2, DROWS, d_product, d_send, d_hold, d_relay, d_recv, dr_send, dr_recv, None
+        d_width, 0, DROWS // 2, DROWS, d_product, d_send, d_hold, d_relay, d_recv, dr_send, dr_recv
     )
     opposite(0)
     beside(0)
@@ -382,14 +377,10 @@
     yt[...] = y_all[row // 8].T
 
     def d_here(c):
-        def body(n, _):
-            cols = pl.ds(al(c * d_width + n * TILE, TILE), TILE)
-            value = d_product(b, cols)
-            mine = yt[pl.ds(al((row % 8) * DROWS, 64), DROWS), :]
-            d_own[:, cols] = value + base[:, cols].astype(F32) + dot(mine, av[:, cols])
-            return 0
-
-        lax.fori_loop(0, d_width // TILE, body, 0)
+        cols = pl.ds(c * d_width, d_width)
+        value = d_product(b, cols)
+        mine = yt[pl.ds(al((row % 8) * DROWS, 64), DROWS), :]
+        d_own[:, cols] = value + base[:, cols].astype(F32) + dot(mine, av[:, cols])
 
     d_here(0)
     relayed(1)
@@ -417,18 +408,32 @@
         copy.wait()
 
 
+def write_out(*refs):
+    ins, outs, held, sem_in, sem_out = refs[:4], refs[4:8], refs[8:12], refs[12], refs[13]
+    reads = [pltpu.make_async_copy(ins[i], held[i], sem_in.at[i]) for i in range(4)]
+    writes = [pltpu.make_async_copy(held[i], outs[i], sem_out.at[i]) for i in range(4)]
+    for copy in reads:
+        copy.start()
+    for read, write in zip(reads, writes):
+        read.wait()
+        write.start()
+    for copy in writes:
+        copy.wait()
+
+
 def per_device(s, r, fw, fr, aw, ar, tip, bw, br):
     hbm = pl.BlockSpec(memory_space=pl.ANY)
     vmem = pltpu.VMEM
     dma = pltpu.SemaphoreType.DMA
+    shapes = (
+        jax.ShapeDtypeStruct((BLOCK, WIN), BF16),
+        jax.ShapeDtypeStruct((ARROW, WIN), BF16),
+        jax.ShapeDtypeStruct((DROWS, WIN), BF16),
+        jax.ShapeDtypeStruct((DROWS, REST), BF16),
+    )
     outs = pl.pallas_call(
         kernel,
-        out_shape=(
-            jax.ShapeDtypeStruct((BLOCK, WIN), BF16),
-            jax.ShapeDtypeStruct((ARROW, WIN), BF16),
-            jax.ShapeDtypeStruct((DROWS, WIN), BF16),
-            jax.ShapeDtypeStruct((DROWS, REST), BF16),
-        ),
+        out_shape=shapes,
         in_specs=[hbm] * 9,
         out_specs=(hbm,) * 4,
         scratch_shapes=[
@@ -474,6 +479,14 @@
         ),
         cost_estimate=pl.CostEstimate(flops=6_800_000_000, bytes_accessed=8_000_000, transcendentals=0),
     )(s[0], r[0].reshape(4, 16, BLOCK), fw[0], fr[0], aw[0], ar[0], tip, bw[0], br[0])
+    outs = pl.pallas_call(
+        write_out,
+        out_shape=shapes,
+        in_specs=[hbm] * 4,
+        out_specs=(hbm,) * 4,
+        scratch_shapes=[vmem(item.shape, BF16) for item in shapes] + [dma((4,)), dma((4,))],
+        compiler_params=pltpu.CompilerParams(vmem_limit_bytes=60 << 20),
+    )(*outs)
     return tuple(value[None] for value in outs)
 
 

time: 99.7 us -> 92 us (0.923)
  local copies, waits for them, and re-layouts: 4.61 us -> 0 us
  Pallas kernels: 93.5 us -> 90.4 us
    unnamed x10 -> x0, local copies, waits for them, and re-layouts: 4.61 us -> none
    pallas_call x1 -> x2, Pallas kernels: 93.5 us -> 90.4 us  [the longest x1 88 us: per_device(): pl.pallas_call(kernel, out_shape=shapes, in_specs=[hbm] * 9, out_specs=(h...]
where the time goes in v2:
time: 92 us; the launch traced here: 91.1 us
  Pallas kernels  90.4 us (98%)
    pallas_call x1, Pallas kernels, per_device(): pl.pallas_call(kernel, out_shape=shapes, in_specs=[hbm] * 9, out_specs=(h...  88 us
    pallas_call x1, Pallas kernels, per_device(): pl.pallas_call(write_out, out_shape=shapes, in_specs=[hbm] * 4, out_specs...  2.4 us

profile of v2, /device:TPU:104, one launch (start us, length us, event | category | flops | bytes accessed | tf_op | source)
XLA Modules:
  0.0 91.1 jit_solution(5206520655395111667)
XLA Ops:
  0.6 88.0 %shard_map.120 = (bf16[256,1536]{1,0:T(8,128)(2,1)}, bf16[64,1536]{1,0:T(8,128)(2,1)}, bf16[192,1536]{1,0:T(8,128)(2,1)}, bf16[192,512]{1,0:T(8,128)(2,1)}) custom-call(bf16[256,2048]{1,0:T(8,128)(2,1)} %bitcast.12, bf16[4,16,256]{2,1,0:T(8,128)(2,1)} %bitcast.23, bf16[256,1536]{1,0:T(8,128)(2,1)} %bitcast.13, bf16[256,512]{1,0:T(8,128)(2,1)} %bitcast.17, ...), custom_call_target="tpu_custom_call" | custom-call | flops 6800000000 | bytes 8000000 | tf_op jit(solution)/shard_map/pallas_call | solution.py:434
  88.7 2.4 %shard_map.121 = (bf16[256,1536]{1,0:T(8,128)(2,1)}, bf16[64,1536]{1,0:T(8,128)(2,1)}, bf16[192,1536]{1,0:T(8,128)(2,1)}, bf16[192,512]{1,0:T(8,128)(2,1)}) custom-call(bf16[256,1536]{1,0:T(8,128)(2,1)} %get-tuple-element.12.refs_0_, bf16[64,1536]{1,0:T(8,128)(2,1)} %get-tuple-element.13.refs_1_, bf16[192,1536]{1,0:T(8,128)(2,1)} %get-tuple-element.14.refs_2_, ...), custom_call_target="tpu_custom_call" | custom-call | tf_op jit(solution)/shard_map/pallas_call | solution.py:482

commit v3 on v2

--- a/solution.py
+++ b/solution.py
@@ -214,44 +214,40 @@
     s_spread(1)
     s_spread(2)
     s_spread(3)
-    f_own(fr_in, WIN, REST, 6)
 
     for copy in locals_:
         copy.wait()
     f_rest_of(0, WIN, 0)
     arrived(sg.at[:, pl.ds(128, 16), :], r_recv)
 
-    def reduce_scatter(width, turn, top, piece, product, send, hold, relay, recv, s_sem, r_sem):
-        def first_of(c):
-            return al((c + turn) % 2 * width, TILE)
-
+    def reduce_scatter(width, top, piece, product, send, hold, relay, recv, s_sem, r_sem):
         def part_of(ref, lead, upper, cols):
             rows = pl.ds(0, top) if upper else pl.ds(top, piece - top)
             return ref.at[lead, rows, cols] if lead is not None else ref.at[rows, cols]
 
         def opposite(c):
-            cols = pl.ds(first_of(c), width)
-            send[0, :, cols] = product(b_opp, cols).astype(BF16)
+            cols = pl.ds(c * width, width)
+            send[0, :, cols] = product(b_opp, c).astype(BF16)
             remote(part_of(send, 0, True, cols), part_of(relay, None, True, cols),
                    s_sem.at[c, 0], r_sem.at[c, 0], at(a, b_next))
             remote(part_of(send, 0, False, cols), part_of(relay, None, False, cols),
                    s_sem.at[c, 1], r_sem.at[c, 1], at(a, b_prev))
 
         def beside(c):
-            cols = pl.ds(first_of(c), width)
-            value = product(b_next, cols)
+            cols = pl.ds(c * width, width)
+            value = product(b_next, c)
             hold[pl.ds(0, top), cols] = value[:top]
             send[1, pl.ds(top, piece - top), cols] = value[top:].astype(BF16)
             remote(part_of(send, 1, False, cols), part_of(recv, 0, False, cols),
                    s_sem.at[c, 2], r_sem.at[c, 2], at(a, b_next))
-            value = product(b_prev, cols)
+            value = product(b_prev, c)
             hold[pl.ds(top, piece - top), cols] = value[top:]
             send[2, pl.ds(0, top), cols] = value[:top].astype(BF16)
             remote(part_of(send, 2, True, cols), part_of(recv, 1, True, cols),
                    s_sem.at[c, 3], r_sem.at[c, 3], at(a, b_prev))
 
         def relayed(c):
-            cols = pl.ds(first_of(c), width)
+            cols = pl.ds(c * width, width)
             arrived(part_of(relay, None, True, cols), r_sem.at[c, 0])
             rows = pl.ds(0, top)
             send[1, rows, cols] = (hold[rows, cols] + relay[rows, cols].astype(F32)).astype(BF16)
@@ -264,7 +260,7 @@
                    s_sem.at[c, 5], r_sem.at[c, 5], at(a, b_prev))
 
         def received(c):
-            cols = pl.ds(first_of(c), width)
+            cols = pl.ds(c * width, width)
             arrived(part_of(recv, 0, False, cols), r_sem.at[c, 2])
             arrived(part_of(recv, 1, True, cols), r_sem.at[c, 3])
             arrived(part_of(recv, 0, True, cols), r_sem.at[c, 4])
@@ -272,61 +268,63 @@
 
         return opposite, beside, relayed, received
 
-    def x_product(b_pos, cols):
-        return dot(sg[b_pos], fg[:, cols])
-
     x_width = 768
+    x_half = 384
+
+    def f_cols(c, part):
+        return pl.ds(al(part * x_width + (c + a) % 2 * x_half, 128), x_half)
+
+    def x_product(b_pos, c):
+        return jnp.concatenate([dot(sg[b_pos], fg[:, f_cols(c, part)]) for part in range(2)], axis=1)
+
     opposite, beside, relayed, received = reduce_scatter(
-        x_width, a, TOP, PIECE, x_product, x_send, x_hold, x_relay, x_recv, xr_send, xr_recv
+        x_width, TOP, PIECE, x_product, x_send, x_hold, x_relay, x_recv, xr_send, xr_recv
     )
 
     def x_here(c):
-        cols = pl.ds(al((c + a) % 2 * x_width, TILE), x_width)
-        value = x_product(b, cols)
-        arrow = lax.dot_general(
-            rz[...].reshape(ARROW, BLOCK), av[:, cols], (((0,), (0,)), ((), ())),
-            preferred_element_type=F32,
-        )
         mine = tip[pl.ds(al(b * 16, 16), 16), :]
-        x_own[pl.ds(0, 128), cols] = value[:128] + arrow[:128]
-        x_own[pl.ds(128, 16), cols] = value[128:TOP] + dot(mine, av[:, cols])
-        x_own[pl.ds(TOP, 128), cols] = value[TOP:] + arrow[128:]
+        ratio = rz[...].reshape(ARROW, BLOCK)
+        for part in range(2):
+            cols = pl.ds(c * x_width + part * x_half, x_half)
+            right = av[:, f_cols(c, part)]
+            value = dot(sg[b], fg[:, f_cols(c, part)])
+            arrow = lax.dot_general(ratio, right, (((0,), (0,)), ((), ())), preferred_element_type=F32)
+            x_own[pl.ds(0, 128), cols] = value[:128] + arrow[:128]
+            x_own[pl.ds(128, 16), cols] = value[128:TOP] + dot(mine, right)
+            x_own[pl.ds(TOP, 128), cols] = value[TOP:] + arrow[128:]
 
     y_rows = pl.ds(al(b * 16, 16), 16)
 
     def x_final(c):
         received(c)
+        if c:
+            f_own(fr_in, WIN, REST, 6)
         turn = (c + a) % 2
-        first = turn * x_width
-
-        def body(n, _):
-            cols = pl.ds(al(first + n * TILE, TILE), TILE)
+        for part in range(2):
+            cols = pl.ds(c * x_width + part * x_half, x_half)
+            into = f_cols(c, part)
             total = x_own[:, cols] + x_recv[0, :, cols].astype(F32) + x_recv[1, :, cols].astype(F32)
             top = total[:128].astype(BF16)
             bottom = total[TOP:].astype(BF16)
-            x_neg[pl.ds(0, 128), cols] = -top
-            x_neg[pl.ds(128, 128), cols] = -bottom
-            xt[cols, pl.ds(0, 128)] = top.T
-            xt[cols, pl.ds(128, 128)] = bottom.T
-            y_all[k, y_rows, cols] = total[128:TOP].astype(BF16)
-            return 0
-
-        lax.fori_loop(0, x_width // TILE, body, 0)
-        y_to = 2 * k + turn
-        here = jnp.logical_and(y_to == y, k == 0)
-        remote_or_local(
-            xt.at[pl.ds(al(first, TILE), x_width), :], xg.at[:, pl.ds(al(y * BLOCK, BLOCK), BLOCK)],
-            xa_send.at[c, 0], xa_recv.at[y], {"row": y_to * 4 + x, "col": 0}, here,
-        )
-        for step in range(4):
-            x_to = (x + step) % 4
-            src = xt.at[pl.ds(al(first + x_to * DROWS, 64), DROWS), :]
-            dst = xg.at[pl.ds(al(y_to * DROWS, 64), DROWS), pl.ds(al(x * BLOCK, BLOCK), BLOCK)]
-            sems = (xa_send.at[c, 1 + step], xa_recv.at[x], {"row": y * 4 + x_to, "col": 1})
-            if step:
-                remote(src, dst, *sems)
-            else:
-                remote_or_local(src, dst, *sems, k == 1)
+            x_neg[pl.ds(0, 128), into] = -top
+            x_neg[pl.ds(128, 128), into] = -bottom
+            xt[into, pl.ds(0, 128)] = top.T
+            xt[into, pl.ds(128, 128)] = bottom.T
+            y_all[k, y_rows, into] = total[128:TOP].astype(BF16)
+            y_to = 2 * k + part
+            remote_or_local(
+                xt.at[into, :], xg.at[pl.ds(al(turn * x_half, 128), x_half), pl.ds(al(y * BLOCK, BLOCK), BLOCK)],
+                xa_send.at[c, part * 3], xa_recv.at[y], {"row": y_to * 4 + x, "col": 0},
+                jnp.logical_and(y_to == y, k == 0),
+            )
+            for step in range(2):
+                x_to = turn * 2 + step
+                remote_or_local(
+                    xt.at[pl.ds(al(part * x_width + x_to * DROWS, 64), DROWS), :],
+                    xg.at[pl.ds(al(y_to * DROWS, 64), DROWS), pl.ds(al(x * BLOCK, BLOCK), BLOCK)],
+                    xa_send.at[c, part * 3 + 1 + step], xa_recv.at[x], {"row": y * 4 + x_to, "col": 1},
+                    jnp.logical_and(x_to == x, k == 1),
+                )
 
     arrived(sg.at[b_opp, pl.ds(0, BLOCK), :], sa_recv.at[b_opp])
     opposite(0)
@@ -334,7 +332,6 @@
     arrived(sg.at[b_prev, pl.ds(0, BLOCK), :], sa_recv.at[b_prev])
     beside(0)
     opposite(1)
-    f_forward(WIN, REST, 6)
     relayed(0)
     beside(1)
     arrived(sg.at[b, pl.ds(0, BLOCK), :], sa_recv.at[b])
@@ -350,19 +347,21 @@
     for step in (1, 2, 3):
         remote(y_mine, y_mine, y_send.at[step - 1], y_recv.at[step - 1], at(a, (b + step) % 4))
 
-    f_rest_of(WIN, REST, 6)
     for a_pos in range(4):
         arrived(xg.at[:, pl.ds(a_pos * BLOCK, BLOCK)], xa_recv.at[a_pos])
 
-    def d_product(b_pos, cols):
-        return dot(xg[pl.ds(al(b_pos * DROWS, 64), DROWS), :], fg[:, cols])
-
     d_width = 1024
+
+    def d_product(b_pos, c):
+        return dot(xg[pl.ds(al(b_pos * DROWS, 64), DROWS), :], fg[:, pl.ds(c * d_width, d_width)])
+
     opposite, beside, relayed, received = reduce_scatter(
-        d_width, 0, DROWS // 2, DROWS, d_product, d_send, d_hold, d_relay, d_recv, dr_send, dr_recv
+        d_width, DROWS // 2, DROWS, d_product, d_send, d_hold, d_relay, d_recv, dr_send, dr_recv
     )
+    f_forward(WIN, REST, 6)
     opposite(0)
     beside(0)
+    f_rest_of(WIN, REST, 6)
     opposite(1)
     for step in (1, 2, 3):
         theirs = y_all.at[k, pl.ds(al(((b + 4 - step) % 4) * 16, 16), 16), :]
@@ -378,7 +377,7 @@
 
     def d_here(c):
         cols = pl.ds(c * d_width, d_width)
-        value = d_product(b, cols)
+        value = d_product(b, c)
         mine = yt[pl.ds(al((row % 8) * DROWS, 64), DROWS), :]
         d_own[:, cols] = value + base[:, cols].astype(F32) + dot(mine, av[:, cols])
 
@@ -468,7 +467,7 @@
             dma((3,)), dma,
             dma((S_CHUNKS, 10)), dma((4,)),
             dma((2, 6)), dma((2, 6)),
-            dma((2, 5)), dma((4,)),
+            dma((2, 6)), dma((4,)),
             dma((3,)), dma((3,)),
             dma, dma,
             dma((2, 6)), dma((2, 6)),

time: 92 us -> 90.4 us (0.983)
  no operation moved by 1% of the time
where the time goes in v3:
time: 90.4 us; the launch traced here: 90.3 us
  Pallas kernels  89.7 us (99%)
    pallas_call x1, Pallas kernels, per_device(): pl.pallas_call(kernel, out_shape=shapes, in_specs=[hbm] * 9, out_specs=(h...  87.3 us
    pallas_call x1, Pallas kernels, per_device(): pl.pallas_call(write_out, out_shape=shapes, in_specs=[hbm] * 4, out_specs...  2.4 us

profile of v3, /device:TPU:104, one launch (start us, length us, event | category | flops | bytes accessed | tf_op | source)
XLA Modules:
  0.0 90.3 jit_solution(16690903711107976125)
XLA Ops:
  0.6 87.3 %shard_map.120 = (bf16[256,1536]{1,0:T(8,128)(2,1)}, bf16[64,1536]{1,0:T(8,128)(2,1)}, bf16[192,1536]{1,0:T(8,128)(2,1)}, bf16[192,512]{1,0:T(8,128)(2,1)}) custom-call(bf16[256,2048]{1,0:T(8,128)(2,1)} %bitcast.12, bf16[4,16,256]{2,1,0:T(8,128)(2,1)} %bitcast.23, bf16[256,1536]{1,0:T(8,128)(2,1)} %bitcast.13, bf16[256,512]{1,0:T(8,128)(2,1)} %bitcast.17, ...), custom_call_target="tpu_custom_call" | custom-call | flops 6800000000 | bytes 8000000 | tf_op jit(solution)/shard_map/pallas_call | solution.py:433
  87.9 2.4 %shard_map.121 = (bf16[256,1536]{1,0:T(8,128)(2,1)}, bf16[64,1536]{1,0:T(8,128)(2,1)}, bf16[192,1536]{1,0:T(8,128)(2,1)}, bf16[192,512]{1,0:T(8,128)(2,1)}) custom-call(bf16[256,1536]{1,0:T(8,128)(2,1)} %get-tuple-element.12.refs_0_, bf16[64,1536]{1,0:T(8,128)(2,1)} %get-tuple-element.13.refs_1_, bf16[192,1536]{1,0:T(8,128)(2,1)} %get-tuple-element.14.refs_2_, ...), custom_call_target="tpu_custom_call" | custom-call | tf_op jit(solution)/shard_map/pallas_call | solution.py:481

commit v4 on v3

--- a/solution.py
+++ b/solution.py
@@ -297,8 +297,6 @@
 
     def x_final(c):
         received(c)
-        if c:
-            f_own(fr_in, WIN, REST, 6)
         turn = (c + a) % 2
         for part in range(2):
             cols = pl.ds(c * x_width + part * x_half, x_half)
@@ -340,6 +338,7 @@
     x_here(1)
     x_final(0)
     x_final(1)
+    f_own(fr_in, WIN, REST, 6)
     outs = [pltpu.make_async_copy(x_neg, x_out, out_sem.at[0])]
     outs[0].start()
 
@@ -358,8 +357,8 @@
     opposite, beside, relayed, received = reduce_scatter(
         d_width, DROWS // 2, DROWS, d_product, d_send, d_hold, d_relay, d_recv, dr_send, dr_recv
     )
+    opposite(0)
     f_forward(WIN, REST, 6)
-    opposite(0)
     beside(0)
     f_rest_of(WIN, REST, 6)
     opposite(1)

time: 90.4 us -> 90.2 us (level)
  Pallas kernels: 89.7 us -> 88.6 us
    pallas_call x1, Pallas kernels: 87.3 us -> 86.2 us  [per_device(): pl.pallas_call(kernel, out_shape=shapes, in_specs=[hbm] * 9, out_specs=(h...]
where the time goes in v4:
time: 90.2 us; the launch traced here: 89.2 us
  Pallas kernels  88.6 us (98%)
    pallas_call x1, Pallas kernels, per_device(): pl.pallas_call(kernel, out_shape=shapes, in_specs=[hbm] * 9, out_specs=(h...  86.2 us
    pallas_call x1, Pallas kernels, per_device(): pl.pallas_call(write_out, out_shape=shapes, in_specs=[hbm] * 4, out_specs...  2.4 us

profile of v4, /device:TPU:104, one launch (start us, length us, event | category | flops | bytes accessed | tf_op | source)
XLA Modules:
  0.0 89.2 jit_solution(4680441501013951209)
XLA Ops:
  0.6 86.2 %shard_map.120 = (bf16[256,1536]{1,0:T(8,128)(2,1)}, bf16[64,1536]{1,0:T(8,128)(2,1)}, bf16[192,1536]{1,0:T(8,128)(2,1)}, bf16[192,512]{1,0:T(8,128)(2,1)}) custom-call(bf16[256,2048]{1,0:T(8,128)(2,1)} %bitcast.12, bf16[4,16,256]{2,1,0:T(8,128)(2,1)} %bitcast.23, bf16[256,1536]{1,0:T(8,128)(2,1)} %bitcast.13, bf16[256,512]{1,0:T(8,128)(2,1)} %bitcast.17, ...), custom_call_target="tpu_custom_call" | custom-call | flops 6800000000 | bytes 8000000 | tf_op jit(solution)/shard_map/pallas_call | solution.py:432
  86.8 2.4 %shard_map.121 = (bf16[256,1536]{1,0:T(8,128)(2,1)}, bf16[64,1536]{1,0:T(8,128)(2,1)}, bf16[192,1536]{1,0:T(8,128)(2,1)}, bf16[192,512]{1,0:T(8,128)(2,1)}) custom-call(bf16[256,1536]{1,0:T(8,128)(2,1)} %get-tuple-element.12.refs_0_, bf16[64,1536]{1,0:T(8,128)(2,1)} %get-tuple-element.13.refs_1_, bf16[192,1536]{1,0:T(8,128)(2,1)} %get-tuple-element.14.refs_2_, ...), custom_call_target="tpu_custom_call" | custom-call | tf_op jit(solution)/shard_map/pallas_call | solution.py:480
